TPU v7x, 256 devices: a whole 4x4x8 slice. The times are simulated.
256 devices in a mesh: vol: 16 (over y, z_hi, core), ctl: 16 (over x, z_lo).
Axes of the slice: x: 4, y: 4, z: 8 (z_hi: 2, z_lo: 4; z = z_hi * 4 + z_lo), core: 2. Of those that a mesh axis runs over, the one named last changes fastest.
Arguments:
- vol_coords: bfloat16 [3, 65536], P(None, ('vol', 'ctl')), may hold values from 0 to 1
- vol_cotangent: bfloat16 [48, 65536], P(None, ('vol', 'ctl')), may hold values from -0.59765625 to 0.59765625
- ctl_coords: bfloat16 [3, 65536], P(None, ('ctl', 'vol')), may hold values from 0 to 1
- ctl_weights: bfloat16 [48, 65536], P(None, ('ctl', 'vol')), may hold values from -0.029907227 to 0.029907227
Outputs:
- weight_grad: float32 [48, 65536], P(None, ('ctl', 'vol'))
- vol_coord_grad: float32 [3, 65536], P(None, ('vol', 'ctl'))
- ctl_coord_grad: float32 [3, 65536], P(None, ('ctl', 'vol'))
All inputs are finite; a program needn't handle non-finite values.
Results may differ from a plain program's by a relative error of at most 0.0028.
Values may be sent and summed in bfloat16 or wider, within the bound.
No kernel may reach another device: no remote copies, remote signals or barrier semaphores. Data moves between devices by JAX's collectives and lax.ppermute only.
A program may use at most 64 MiB of HBM per device.

v0:
```python
import math

import jax
import jax.numpy as jnp
from jax import lax
from jax.sharding import PartitionSpec as P

support_radius = 0.25
slope_factor = -20.0 / (0.25 * 0.25)


def tile_terms(vol_xyz, vol_cot, ctl_xyz, ctl_wts):
    vol_pos = vol_xyz.astype(jnp.float32)
    ctl_pos = ctl_xyz.astype(jnp.float32)
    squared = jnp.zeros((vol_pos.shape[1], ctl_pos.shape[1]), jnp.float32)
    for component in range(3):
        offset = vol_pos[component][:, None] - ctl_pos[component][None, :]
        squared = squared + offset * offset
    ratio = jnp.sqrt(squared) / support_radius
    inside = jnp.maximum(1.0 - ratio, 0.0)
    cubic_term = inside * inside * inside
    kernel = (cubic_term * inside * (4.0 * ratio + 1.0)).astype(jnp.bfloat16)
    pair_dot = lax.dot_general(
        vol_cot, ctl_wts, (((0,), (0,)), ((), ())), preferred_element_type=jnp.float32
    )
    weighting = slope_factor * cubic_term * pair_dot
    weight_grad = jnp.dot(vol_cot, kernel, preferred_element_type=jnp.float32)
    row_total = jnp.sum(weighting, axis=1)
    col_total = jnp.sum(weighting, axis=0)
    pulled = lax.dot_general(
        ctl_pos,
        weighting,
        (((1,), (1,)), ((), ())),
        precision=lax.Precision.HIGHEST,
        preferred_element_type=jnp.float32,
    )
    pushed = jnp.dot(
        vol_pos, weighting, precision=lax.Precision.HIGHEST, preferred_element_type=jnp.float32
    )
    vol_grad = vol_pos * row_total[None, :] - pulled
    ctl_grad = ctl_pos * col_total[None, :] - pushed
    return (vol_grad, weight_grad, ctl_grad)


def sweep(vol_xyz, vol_cot, ctl_xyz, ctl_wts, limit):
    vol_count = vol_xyz.shape[1]
    ctl_count = ctl_xyz.shape[1]
    block_len = math.gcd(vol_count, limit)
    blocks = vol_count // block_len
    stacked_xyz = vol_xyz.reshape(3, blocks, block_len).transpose(1, 0, 2)
    stacked_cot = vol_cot.reshape(vol_cot.shape[0], blocks, block_len).transpose(1, 0, 2)

    def advance(carry, items):
        xyz_block, cot_block = items
        vol_grad, weight_grad, ctl_grad = tile_terms(xyz_block, cot_block, ctl_xyz, ctl_wts)
        return ((carry[0] + weight_grad, carry[1] + ctl_grad), vol_grad)

    start_carry = (
        jnp.zeros((vol_cot.shape[0], ctl_count), jnp.float32),
        jnp.zeros((3, ctl_count), jnp.float32),
    )
    totals, vol_parts = lax.scan(advance, start_carry, (stacked_xyz, stacked_cot))
    vol_grad = vol_parts.transpose(1, 0, 2).reshape(3, vol_count)
    return (vol_grad, totals[0], totals[1])


def shards(vol_coords, vol_cotangent, ctl_coords, ctl_weights):
    all_xyz, all_cot = (
        lax.all_gather(vol_coords, "ctl", axis=1, tiled=True),
        lax.all_gather(vol_cotangent, "ctl", axis=1, tiled=True),
    )
    piece_xyz = lax.all_gather(ctl_coords, "vol", axis=1, tiled=True)
    piece_wts = lax.all_gather(ctl_weights, "vol", axis=1, tiled=True)
    vol_grad, weight_grad, ctl_grad = sweep(all_xyz, all_cot, piece_xyz, piece_wts, 512)
    vol_grad, weight_grad, ctl_grad = (vol_grad, weight_grad, ctl_grad)
    weight_part, ctl_part = (
        lax.psum_scatter(weight_grad, "vol", scatter_dimension=1, tiled=True),
        lax.psum_scatter(ctl_grad, "vol", scatter_dimension=1, tiled=True),
    )
    vol_part = lax.psum_scatter(vol_grad, "ctl", scatter_dimension=1, tiled=True)
    return (weight_part, vol_part, ctl_part)


def solution(mesh):
    in_specs = (
        P(None, ("vol", "ctl")),
        P(None, ("vol", "ctl")),
        P(None, ("ctl", "vol")),
        P(None, ("ctl", "vol")),
    )
    out_specs = (P(None, ("ctl", "vol")), P(None, ("vol", "ctl")), P(None, ("ctl", "vol")))
    return jax.shard_map(shards, mesh=mesh, in_specs=in_specs, out_specs=out_specs, check_vma=False)
```

profile of v0, /device:TPU:8, one launch (start us, length us, event | category | flops | bytes accessed | tf_op | source)
XLA Modules:
  0.0 578.8 jit_solution(1203335255077515208)
XLA Ops:
  7.2 44.0 %all_gather.13 = bf16[3,4096]{1,0:T(4,128)(2,1)S(1)} all-gather(bf16[3,256]{1,0:T(4,128)(2,1)} %param.6), channel_id=1, replica_groups=mesh['vol'=16,'ctl'=16] {'ctl'}, dimensions={1}, use_global_device_ids=true | all-gather | bytes 26112 | tf_op jit(solution)/shard_map/all_gather | solution.py:69
  51.2 28.8 %all_gather.14 = bf16[3,4096]{1,0:T(4,128)(2,1)S(1)} all-gather(bf16[3,256]{1,0:T(4,128)(2,1)} %param.8), channel_id=1, replica_groups=mesh['vol'=16,'ctl'=16] {'vol'}, dimensions={1}, use_global_device_ids=true | all-gather | bytes 26112 | tf_op jit(solution)/shard_map/all_gather | solution.py:72
  80.0 40.6 %all_gather.12 = bf16[48,4096]{1,0:T(8,128)(2,1)S(1)} all-gather(bf16[48,256]{1,0:T(8,128)(2,1)} %param.7), channel_id=1, replica_groups=mesh['vol'=16,'ctl'=16] {'ctl'}, dimensions={1}, use_global_device_ids=true | all-gather | bytes 417792 | tf_op jit(solution)/shard_map/all_gather | solution.py:70
  120.8 27.1 %all_gather.15 = bf16[48,4096]{1,0:T(8,128)(2,1)S(1)} all-gather(bf16[48,256]{1,0:T(8,128)(2,1)} %param.9), channel_id=1, replica_groups=mesh['vol'=16,'ctl'=16] {'vol'}, dimensions={1}, use_global_device_ids=true | all-gather | bytes 417792 | tf_op jit(solution)/shard_map/all_gather | solution.py:73
  147.9 167.3 %while.17 = (s32[]{:T(128)}, f32[48,4096]{1,0:T(8,128)S(1)}, f32[3,4096]{1,0:T(4,128)S(1)}, f32[8,3,512]{2,1,0:T(4,128)S(1)}, bf16[8,48,512]{2,1,0:T(8,128)(2,1)...) while((s32[]{:T(128)}, f32[48,4096]{1,0:T(8,128)S(1)}, ...), condition=%wide.region_3.4_spmd.clone, body=%wide.region_0.3_spmd.clone.sunk | while | flops 627504640 | bytes 27694220 | solution.py:62
  148.0 7.0 %convolution_add_fusion.2 = f32[48,4096]{1,0:T(8,128)S(1)} fusion(f32[4096]{0:T(1024)S(1)} %bitcast.91, f32[512]{0:T(512)S(1)} %bitcast.99, f32[4096]{0:T(1024)S(1)} %bitcast.89, f32[512]{0:T(512)S(1)} %bitcast.101, f32[4096]{0:T(1024)S(1)} %bitcast.87, f32[512]{0:T(512)S(1)} %bitcast.97, f32[48,4096]{1,0:T(8,128)S(1)} %get-tuple-element.255, ...), kind=kOutput, calls=%fused_computation.8.clone.1 | convolution fusion | flops 239468544 | bytes 1677317 | tf_op jit(solution)/shard_map/while/body/eval_jaxpr/dot_general | solution.py:27
  155.0 6.8 %fusion.60 = (f32[512]{0:T(512)S(1)}, f32[4096]{0:T(1024)S(1)}, f32[512,4096]{1,0:T(8,128)S(1)}) fusion(bf16[48,4096]{1,0:T(8,128)(2,1)S(1)} %get-tuple-element.271, bf16[8,48,512]{2,1,0:T(8,128)(2,1)S(1)} %get-tuple-element.268, s32[]{:T(128)S(6)} %copy.22, f32[4096]{0:T(1024)S(1)} %bitcast.92, f32[512]{0:T(512)S(1)} %bitcast.100, ...), kind=kOutput, calls=%fused_computation.38.clone.1 | convolution fusion | flops 236973568 | bytes 8904708 | tf_op jit(solution)/shard_map/while/body/eval_jaxpr/dot_general | solution.py:23
  164.8 4.0 fusion.62
  168.9 7.0 %convolution_add_fusion.2 = f32[48,4096]{1,0:T(8,128)S(1)} fusion(f32[4096]{0:T(1024)S(1)} %bitcast.91, f32[512]{0:T(512)S(1)} %bitcast.99, f32[4096]{0:T(1024)S(1)} %bitcast.89, f32[512]{0:T(512)S(1)} %bitcast.101, f32[4096]{0:T(1024)S(1)} %bitcast.87, f32[512]{0:T(512)S(1)} %bitcast.97, f32[48,4096]{1,0:T(8,128)S(1)} %get-tuple-element.255, ...), kind=kOutput, calls=%fused_computation.8.clone.1 | convolution fusion | flops 239468544 | bytes 1677317 | tf_op jit(solution)/shard_map/while/body/eval_jaxpr/dot_general | solution.py:27
  175.9 6.8 %fusion.60 = (f32[512]{0:T(512)S(1)}, f32[4096]{0:T(1024)S(1)}, f32[512,4096]{1,0:T(8,128)S(1)}) fusion(bf16[48,4096]{1,0:T(8,128)(2,1)S(1)} %get-tuple-element.271, bf16[8,48,512]{2,1,0:T(8,128)(2,1)S(1)} %get-tuple-element.268, s32[]{:T(128)S(6)} %copy.22, f32[4096]{0:T(1024)S(1)} %bitcast.92, f32[512]{0:T(512)S(1)} %bitcast.100, ...), kind=kOutput, calls=%fused_computation.38.clone.1 | convolution fusion | flops 236973568 | bytes 8904708 | tf_op jit(solution)/shard_map/while/body/eval_jaxpr/dot_general | solution.py:23
  185.7 4.0 fusion.62
  189.8 7.0 %convolution_add_fusion.2 = f32[48,4096]{1,0:T(8,128)S(1)} fusion(f32[4096]{0:T(1024)S(1)} %bitcast.91, f32[512]{0:T(512)S(1)} %bitcast.99, f32[4096]{0:T(1024)S(1)} %bitcast.89, f32[512]{0:T(512)S(1)} %bitcast.101, f32[4096]{0:T(1024)S(1)} %bitcast.87, f32[512]{0:T(512)S(1)} %bitcast.97, f32[48,4096]{1,0:T(8,128)S(1)} %get-tuple-element.255, ...), kind=kOutput, calls=%fused_computation.8.clone.1 | convolution fusion | flops 239468544 | bytes 1677317 | tf_op jit(solution)/shard_map/while/body/eval_jaxpr/dot_general | solution.py:27
  196.8 6.8 %fusion.60 = (f32[512]{0:T(512)S(1)}, f32[4096]{0:T(1024)S(1)}, f32[512,4096]{1,0:T(8,128)S(1)}) fusion(bf16[48,4096]{1,0:T(8,128)(2,1)S(1)} %get-tuple-element.271, bf16[8,48,512]{2,1,0:T(8,128)(2,1)S(1)} %get-tuple-element.268, s32[]{:T(128)S(6)} %copy.22, f32[4096]{0:T(1024)S(1)} %bitcast.92, f32[512]{0:T(512)S(1)} %bitcast.100, ...), kind=kOutput, calls=%fused_computation.38.clone.1 | convolution fusion | flops 236973568 | bytes 8904708 | tf_op jit(solution)/shard_map/while/body/eval_jaxpr/dot_general | solution.py:23
  206.6 4.0 fusion.62
  210.7 7.0 %convolution_add_fusion.2 = f32[48,4096]{1,0:T(8,128)S(1)} fusion(f32[4096]{0:T(1024)S(1)} %bitcast.91, f32[512]{0:T(512)S(1)} %bitcast.99, f32[4096]{0:T(1024)S(1)} %bitcast.89, f32[512]{0:T(512)S(1)} %bitcast.101, f32[4096]{0:T(1024)S(1)} %bitcast.87, f32[512]{0:T(512)S(1)} %bitcast.97, f32[48,4096]{1,0:T(8,128)S(1)} %get-tuple-element.255, ...), kind=kOutput, calls=%fused_computation.8.clone.1 | convolution fusion | flops 239468544 | bytes 1677317 | tf_op jit(solution)/shard_map/while/body/eval_jaxpr/dot_general | solution.py:27
  217.7 6.8 %fusion.60 = (f32[512]{0:T(512)S(1)}, f32[4096]{0:T(1024)S(1)}, f32[512,4096]{1,0:T(8,128)S(1)}) fusion(bf16[48,4096]{1,0:T(8,128)(2,1)S(1)} %get-tuple-element.271, bf16[8,48,512]{2,1,0:T(8,128)(2,1)S(1)} %get-tuple-element.268, s32[]{:T(128)S(6)} %copy.22, f32[4096]{0:T(1024)S(1)} %bitcast.92, f32[512]{0:T(512)S(1)} %bitcast.100, ...), kind=kOutput, calls=%fused_computation.38.clone.1 | convolution fusion | flops 236973568 | bytes 8904708 | tf_op jit(solution)/shard_map/while/body/eval_jaxpr/dot_general | solution.py:23
  227.5 4.0 fusion.62
  231.6 7.0 %convolution_add_fusion.2 = f32[48,4096]{1,0:T(8,128)S(1)} fusion(f32[4096]{0:T(1024)S(1)} %bitcast.91, f32[512]{0:T(512)S(1)} %bitcast.99, f32[4096]{0:T(1024)S(1)} %bitcast.89, f32[512]{0:T(512)S(1)} %bitcast.101, f32[4096]{0:T(1024)S(1)} %bitcast.87, f32[512]{0:T(512)S(1)} %bitcast.97, f32[48,4096]{1,0:T(8,128)S(1)} %get-tuple-element.255, ...), kind=kOutput, calls=%fused_computation.8.clone.1 | convolution fusion | flops 239468544 | bytes 1677317 | tf_op jit(solution)/shard_map/while/body/eval_jaxpr/dot_general | solution.py:27
  238.6 6.8 %fusion.60 = (f32[512]{0:T(512)S(1)}, f32[4096]{0:T(1024)S(1)}, f32[512,4096]{1,0:T(8,128)S(1)}) fusion(bf16[48,4096]{1,0:T(8,128)(2,1)S(1)} %get-tuple-element.271, bf16[8,48,512]{2,1,0:T(8,128)(2,1)S(1)} %get-tuple-element.268, s32[]{:T(128)S(6)} %copy.22, f32[4096]{0:T(1024)S(1)} %bitcast.92, f32[512]{0:T(512)S(1)} %bitcast.100, ...), kind=kOutput, calls=%fused_computation.38.clone.1 | convolution fusion | flops 236973568 | bytes 8904708 | tf_op jit(solution)/shard_map/while/body/eval_jaxpr/dot_general | solution.py:23
  248.4 4.0 fusion.62
  252.5 7.0 %convolution_add_fusion.2 = f32[48,4096]{1,0:T(8,128)S(1)} fusion(f32[4096]{0:T(1024)S(1)} %bitcast.91, f32[512]{0:T(512)S(1)} %bitcast.99, f32[4096]{0:T(1024)S(1)} %bitcast.89, f32[512]{0:T(512)S(1)} %bitcast.101, f32[4096]{0:T(1024)S(1)} %bitcast.87, f32[512]{0:T(512)S(1)} %bitcast.97, f32[48,4096]{1,0:T(8,128)S(1)} %get-tuple-element.255, ...), kind=kOutput, calls=%fused_computation.8.clone.1 | convolution fusion | flops 239468544 | bytes 1677317 | tf_op jit(solution)/shard_map/while/body/eval_jaxpr/dot_general | solution.py:27
  259.5 6.8 %fusion.60 = (f32[512]{0:T(512)S(1)}, f32[4096]{0:T(1024)S(1)}, f32[512,4096]{1,0:T(8,128)S(1)}) fusion(bf16[48,4096]{1,0:T(8,128)(2,1)S(1)} %get-tuple-element.271, bf16[8,48,512]{2,1,0:T(8,128)(2,1)S(1)} %get-tuple-element.268, s32[]{:T(128)S(6)} %copy.22, f32[4096]{0:T(1024)S(1)} %bitcast.92, f32[512]{0:T(512)S(1)} %bitcast.100, ...), kind=kOutput, calls=%fused_computation.38.clone.1 | convolution fusion | flops 236973568 | bytes 8904708 | tf_op jit(solution)/shard_map/while/body/eval_jaxpr/dot_general | solution.py:23
  269.3 4.0 fusion.62
  273.4 7.0 %convolution_add_fusion.2 = f32[48,4096]{1,0:T(8,128)S(1)} fusion(f32[4096]{0:T(1024)S(1)} %bitcast.91, f32[512]{0:T(512)S(1)} %bitcast.99, f32[4096]{0:T(1024)S(1)} %bitcast.89, f32[512]{0:T(512)S(1)} %bitcast.101, f32[4096]{0:T(1024)S(1)} %bitcast.87, f32[512]{0:T(512)S(1)} %bitcast.97, f32[48,4096]{1,0:T(8,128)S(1)} %get-tuple-element.255, ...), kind=kOutput, calls=%fused_computation.8.clone.1 | convolution fusion | flops 239468544 | bytes 1677317 | tf_op jit(solution)/shard_map/while/body/eval_jaxpr/dot_general | solution.py:27
  280.4 6.8 %fusion.60 = (f32[512]{0:T(512)S(1)}, f32[4096]{0:T(1024)S(1)}, f32[512,4096]{1,0:T(8,128)S(1)}) fusion(bf16[48,4096]{1,0:T(8,128)(2,1)S(1)} %get-tuple-element.271, bf16[8,48,512]{2,1,0:T(8,128)(2,1)S(1)} %get-tuple-element.268, s32[]{:T(128)S(6)} %copy.22, f32[4096]{0:T(1024)S(1)} %bitcast.92, f32[512]{0:T(512)S(1)} %bitcast.100, ...), kind=kOutput, calls=%fused_computation.38.clone.1 | convolution fusion | flops 236973568 | bytes 8904708 | tf_op jit(solution)/shard_map/while/body/eval_jaxpr/dot_general | solution.py:23
  290.3 4.0 fusion.62
  294.3 7.0 %convolution_add_fusion.2 = f32[48,4096]{1,0:T(8,128)S(1)} fusion(f32[4096]{0:T(1024)S(1)} %bitcast.91, f32[512]{0:T(512)S(1)} %bitcast.99, f32[4096]{0:T(1024)S(1)} %bitcast.89, f32[512]{0:T(512)S(1)} %bitcast.101, f32[4096]{0:T(1024)S(1)} %bitcast.87, f32[512]{0:T(512)S(1)} %bitcast.97, f32[48,4096]{1,0:T(8,128)S(1)} %get-tuple-element.255, ...), kind=kOutput, calls=%fused_computation.8.clone.1 | convolution fusion | flops 239468544 | bytes 1677317 | tf_op jit(solution)/shard_map/while/body/eval_jaxpr/dot_general | solution.py:27
  301.4 6.8 %fusion.60 = (f32[512]{0:T(512)S(1)}, f32[4096]{0:T(1024)S(1)}, f32[512,4096]{1,0:T(8,128)S(1)}) fusion(bf16[48,4096]{1,0:T(8,128)(2,1)S(1)} %get-tuple-element.271, bf16[8,48,512]{2,1,0:T(8,128)(2,1)S(1)} %get-tuple-element.268, s32[]{:T(128)S(6)} %copy.22, f32[4096]{0:T(1024)S(1)} %bitcast.92, f32[512]{0:T(512)S(1)} %bitcast.100, ...), kind=kOutput, calls=%fused_computation.38.clone.1 | convolution fusion | flops 236973568 | bytes 8904708 | tf_op jit(solution)/shard_map/while/body/eval_jaxpr/dot_general | solution.py:23
  311.2 4.0 fusion.62
  320.0 82.6 %reduce-scatter.12.cloned.1.call-done = f32[256,3]{1,0:T(8,128)} async-done(((f32[4096,3]{1,0:T(8,128)}), f32[256,3]{1,0:T(8,128)}) %reduce-scatter.12.cloned.1.call-update) | async-done | bytes 3088
  404.2 89.1 %reduce-scatter.10.cloned.1.call-done = f32[256,3]{1,0:T(8,128)} async-done(((f32[4096,3]{1,0:T(8,128)}), f32[256,3]{1,0:T(8,128)}) %reduce-scatter.10.cloned.1.call-update) | async-done | bytes 3088
  494.8 77.4 %reduce-scatter.8.cloned.1.call-done = f32[48,256]{1,0:T(8,128)} async-done(((f32[48,4096]{1,0:T(8,128)}), f32[48,256]{1,0:T(8,128)}) %reduce-scatter.8.cloned.1.call-update) | async-done | bytes 49168 | tf_op jit(solution)/shard_map/reduce_scatter | solution.py:77
  (49 shorter events, 32.5 us)
Async XLA Ops:
  7.2 395.4 %reduce-scatter.12.cloned.1.call-start = ((), (), s32[]{:S(2)}) async-start(), calls=%async_computation.5 | async-start | bytes 2228224
  315.2 4.1 copy-start
  317.1 176.1 %reduce-scatter.10.cloned.1.call-start = ((), (), s32[]{:S(2)}) async-start(), calls=%async_computation.4 | async-start | bytes 2228224
  319.2 253.0 %reduce-scatter.8.cloned.1.call-start = ((), (), s32[]{:S(2)}) async-start(), calls=%async_computation.3 | async-start | bytes 835584 | tf_op jit(solution)/shard_map/reduce_scatter | solution.py:77
Sparse Core Ops, SparseCore 0:
  317.3 85.2 reduce-scatter.11
  405.1 88.1 reduce-scatter.9
  497.9 74.3 reduce-scatter.7
where the time goes:
time: 579 us
  waiting for transfers between devices  250 us (43%)
  matrix products  167 us (29%)
  blocking collectives  140 us (24%)
  between operations  13.8 us (2%)
  local copies, waits for them, and re-layouts  7.7 us (1%)
    unnamed x5, waiting for transfers between devices  172 us
    reduce_scatter x1, waiting for transfers between devices, shards(): lax.psum_scatter(weight_grad, 'vol', scatter_dimension=1, tiled=True)  77.4 us
    dot_general x8, matrix products, tile_terms(): weight_grad = jnp.dot(vol_cot, kernel, preferred_element_type=jnp.float32)  56.2 us
    dot_general x8, matrix products, tile_terms(): lax.dot_general(vol_cot, ctl_wts, (((0,), (0,)), ((), ())), preferred_ele...  54.6 us
    all_gather x1, blocking collectives, shards(): lax.all_gather(vol_coords, 'ctl', axis=1, tiled=True)  44 us
    all_gather x1, blocking collectives, shards(): lax.all_gather(vol_cotangent, 'ctl', axis=1, tiled=True)  40.6 us
    dot_general x8, matrix products, tile_terms(): lax.dot_general(ctl_pos, weighting, (((1,), (1,)), ((), ())), precision=l...  31.9 us
    all_gather x1, blocking collectives, shards(): piece_xyz = lax.all_gather(ctl_coords, 'vol', axis=1, tiled=True)  28.8 us
  transfers between devices with their start and end apart: 3, of which 3 were waited for; matrix products, arithmetic and copies ran while one was open for 1% of the time, Pallas kernels for 0%

commit v1 on v0

v1 whole, which is shorter than its diff:
```python
import jax
import jax.numpy as jnp
from jax import lax
from jax.experimental import pallas as pl
from jax.experimental.pallas import tpu as pltpu
from jax.sharding import PartitionSpec as P

F32 = jnp.float32
BF = jnp.bfloat16
VMEM = pltpu.VMEM
WIDE = 64
BLOCK = 256
SLOPE = -320.0


def split3(total):
    first = total.astype(BF)
    rest = total - first.astype(F32)
    second = rest.astype(BF)
    third = (rest - second.astype(F32)).astype(BF)
    return (first, second, third)


def pack_kernel(vx_ref, vc_ref, cx_ref, cw_ref, v_ref, c_ref):
    ones = jnp.ones((3, BLOCK), BF)
    blank = jnp.zeros((7, BLOCK), BF)
    v = vx_ref[...].astype(F32) * 4.0
    v_len = jnp.concatenate(split3(jnp.sum(v * v, axis=0, keepdims=True)), axis=0)
    v_ref[0:48, :] = vc_ref[...]
    v_ref[48:64, :] = jnp.concatenate([(v * -2.0).astype(BF), v_len, ones, blank], axis=0)
    c = cx_ref[...].astype(F32) * 4.0
    c_len = jnp.concatenate(split3(jnp.sum(c * c, axis=0, keepdims=True)), axis=0)
    c_ref[0:48, :] = cw_ref[...]
    c_ref[48:64, :] = jnp.concatenate([c.astype(BF), ones, c_len, blank], axis=0)


def pack(vol_coords, vol_cotangent, ctl_coords, ctl_weights):
    packed = jax.ShapeDtypeStruct((WIDE, BLOCK), BF)
    return pl.pallas_call(
        pack_kernel,
        out_shape=(packed, packed),
        in_specs=[pl.BlockSpec(memory_space=VMEM)] * 4,
        out_specs=[pl.BlockSpec(memory_space=VMEM)] * 2,
    )(vol_coords, vol_cotangent, ctl_coords, ctl_weights)


def pair_kernel(*refs):
    v_parts = refs[0:4]
    c_parts = refs[4:12]
    c_out, v_out, v_all, v_tall, c_all, c_two, v_sum = refs[12:]
    for part in range(4):
        for slot in range(4):
            at = (part * 4 + slot) * BLOCK
            block = v_parts[part][slot]
            v_all[:, at : at + BLOCK] = block
            v_tall[at : at + BLOCK, :] = block.T
    rows = lax.broadcasted_iota(jnp.int32, (WIDE, BLOCK), 0)
    for part in range(8):
        for slot in range(2):
            block = c_parts[part][slot]
            blank = jnp.zeros_like(block)
            c_all[part * 2 + slot] = block
            c_two[part * 2 + slot, :, :BLOCK] = jnp.where(rows >= 48, block, blank)
            c_two[part * 2 + slot, :, BLOCK:] = jnp.where(rows < 48, block, blank)
    v_sum[...] = jnp.zeros_like(v_sum)

    def tile(n, carry):
        both = jnp.dot(v_tall[...], c_two[n], preferred_element_type=F32)
        squared = jnp.maximum(both[:, :BLOCK], 1e-20)
        pair_dot = both[:, BLOCK:]
        inside = jnp.maximum(1.0 - squared * lax.rsqrt(squared), 0.0)
        second = inside * inside
        kernel = (second * second * (inside - 1.25)).astype(BF)
        weighting = (second * inside * pair_dot).astype(BF)
        weight_grad = jnp.dot(v_all[0:48, :], kernel, preferred_element_type=F32)
        pushed = jnp.dot(v_all[48:64, :], weighting, preferred_element_type=F32)
        own = c_all[n, 48:64, :]
        v_sum[...] += lax.dot_general(
            own, weighting, (((1,), (1,)), ((), ())), preferred_element_type=F32
        )
        c_out[n, 0:48, :] = weight_grad * -4.0
        ctl_pos = own[0:3].astype(F32) * 0.25
        grad = (ctl_pos * pushed[6:7] + pushed[0:3] * 0.125) * SLOPE
        c_out[n, 48:56, :] = jnp.concatenate([grad, jnp.zeros((5, BLOCK), F32)], axis=0)
        return carry

    lax.fori_loop(0, 16, tile, 0)
    for n in range(16):
        at = n * BLOCK
        pulled = v_sum[:, at : at + BLOCK]
        vol_pos = v_all[48:64, at : at + BLOCK][0:3].astype(F32) * -0.125
        grad = (vol_pos * pulled[3:4] - pulled[0:3] * 0.25) * SLOPE
        v_out[n] = jnp.concatenate([grad, jnp.zeros((5, BLOCK), F32)], axis=0)


def pair_sums(v_parts, c_parts):
    return pl.pallas_call(
        pair_kernel,
        out_shape=(
            jax.ShapeDtypeStruct((16, 56, BLOCK), F32),
            jax.ShapeDtypeStruct((16, 8, BLOCK), F32),
        ),
        in_specs=[pl.BlockSpec(memory_space=VMEM)] * 12,
        out_specs=[pl.BlockSpec(memory_space=VMEM)] * 2,
        scratch_shapes=[
            VMEM((WIDE, 16 * BLOCK), BF),
            VMEM((16 * BLOCK, WIDE), BF),
            VMEM((16, WIDE, BLOCK), BF),
            VMEM((16, WIDE, 2 * BLOCK), BF),
            VMEM((16, 16 * BLOCK), F32),
        ],
        compiler_params=pltpu.CompilerParams(vmem_limit_bytes=48 * 2**20),
        cost_estimate=pl.CostEstimate(flops=10**10, bytes_accessed=4 * 10**6, transcendentals=0),
    )(*v_parts, *c_parts)


def send(value, axis, target):
    return lax.ppermute(value, axis, [(i, target(i)) for i in range(16)])


def near(step):
    return lambda i: i // 4 * 4 + (i + step) % 4


def far(step):
    return lambda i: (i + 4 * step) % 16


def shards(vol_coords, vol_cotangent, ctl_coords, ctl_weights):
    v, c = pack(vol_coords, vol_cotangent, ctl_coords, ctl_weights)
    core = lambda i: i ^ 1
    half = lambda i: i ^ 2
    v_line = jnp.stack([v] + [send(v, "ctl", near(s)) for s in (1, 2, 3)])
    c_pair = jnp.stack([c, send(c, "vol", half)])
    v_parts = [v_line] + [send(v_line, "ctl", far(s)) for s in (1, 2, 3)]
    c_parts = [c_pair] + [send(c_pair, "vol", far(s)) for s in (1, 2, 3)]
    c_parts = c_parts + [send(part, "vol", core) for part in c_parts]
    c_out, v_out = pair_sums(v_parts, c_parts)
    c_sum = c_out[:8] + send(c_out[8:], "vol", core)
    c_back = [send(c_sum[2 * s : 2 * s + 2], "vol", far(-s)) for s in (1, 2, 3)]
    v_back = [send(v_out[4 * s : 4 * s + 4], "ctl", far(-s)) for s in (1, 2, 3)]
    c_sum = c_sum[:2] + c_back[0] + c_back[1] + c_back[2]
    v_sum = v_out[:4] + v_back[0] + v_back[1] + v_back[2]
    c_sum = c_sum[0] + send(c_sum[1], "vol", half)
    v_last = [send(v_sum[s], "ctl", near(-s)) for s in (1, 2, 3)]
    v_sum = v_sum[0] + v_last[0] + v_last[1] + v_last[2]
    return (c_sum[0:48], v_sum[0:3], c_sum[48:51])


def solution(mesh):
    in_specs = (
        P(None, ("vol", "ctl")),
        P(None, ("vol", "ctl")),
        P(None, ("ctl", "vol")),
        P(None, ("ctl", "vol")),
    )
    out_specs = (P(None, ("ctl", "vol")), P(None, ("vol", "ctl")), P(None, ("ctl", "vol")))
    return jax.shard_map(shards, mesh=mesh, in_specs=in_specs, out_specs=out_specs, check_vma=False)
```

time: 579 us -> 105 us (0.18)
  waiting for transfers between devices: 250 us -> 15.2 us
  matrix products: 167 us -> 0 us
  blocking collectives: 140 us -> 0 us
  Pallas kernels: 0 us -> 47.2 us
  starting transfers between devices: 0.12 us -> 38.4 us
  between operations: 13.8 us -> 0.73 us
  local copies, waits for them, and re-layouts: 7.7 us -> 1.29 us
    unnamed x5 -> x0, waiting for transfers between devices: 172 us -> none
    dot_general x32 -> x0, matrix products: 167 us -> none  [the longest x8 56.2 us: tile_terms(): weight_grad = jnp.dot(vol_cot, kernel, preferred_element_type=jnp.float32)]
    all_gather x4 -> x0, blocking collectives: 140 us -> none  [the longest x1 44 us: shards(): lax.all_gather(vol_coords, 'ctl', axis=1, tiled=True)]
    reduce_scatter x1 -> x0, waiting for transfers between devices: 77.4 us -> none  [shards(): lax.psum_scatter(weight_grad, 'vol', scatter_dimension=1, tiled=True)]
    pallas_call x0 -> x2, Pallas kernels: none -> 47.2 us  [the longest x1 45.7 us: pair_sums(): pl.pallas_call(pair_kernel, out_shape=(jax.ShapeDtypeStruct((16, 56, BLOC...]
    ppermute x0 -> x25, starting transfers between devices: none -> 38.4 us  [send(): return lax.ppermute(value, axis, [(i, target(i)) for i in range(16)])]
    ppermute x0 -> x25, waiting for transfers between devices: none -> 15.2 us  [send(): return lax.ppermute(value, axis, [(i, target(i)) for i in range(16)])]
    unnamed x8 -> x2, local copies, waits for them, and re-layouts: 7.35 us -> 0.01 us
  transfers between devices with their start and end apart: 3 -> 25, of which waited for: 3 -> 9; matrix products, arithmetic and copies ran while one was open for 1% -> 1% of each run, Pallas kernels for 0% -> 0%
where the time goes in v1:
time: 105 us; the launch traced here: 104 us
  Pallas kernels  47.2 us (45%)
  starting transfers between devices  38.4 us (37%)
  waiting for transfers between devices  15.2 us (14%)
  other arithmetic  1.5 us (1%)
  local copies, waits for them, and re-layouts  1.29 us (1%)
    pallas_call x1, Pallas kernels, pair_sums(): pl.pallas_call(pair_kernel, out_shape=(jax.ShapeDtypeStruct((16, 56, BLOC...  45.7 us
    ppermute x25, starting transfers between devices, send(): return lax.ppermute(value, axis, [(i, target(i)) for i in range(16)])  38.4 us
    ppermute x25, waiting for transfers between devices, send(): return lax.ppermute(value, axis, [(i, target(i)) for i in range(16)])  15.2 us
  transfers between devices with their start and end apart: 25, of which 9 were waited for; matrix products, arithmetic and copies ran while one was open for 1% of the time, Pallas kernels for 0%

profile of v1, /device:TPU:8, one launch (start us, length us, event | category | flops | bytes accessed | tf_op | source)
XLA Modules:
  0.0 104.2 jit_solution(7625629123533172212)
XLA Ops:
  0.6 1.4 %shard_map.67 = (bf16[64,256]{1,0:T(8,128)(2,1)}, bf16[64,256]{1,0:T(8,128)(2,1)}) custom-call(bf16[3,256]{1,0:T(4,128)(2,1)} %vx_ref.1, bf16[48,256]{1,0:T(8,128)(2,1)} %vc_ref.1, bf16[3,256]{1,0:T(4,128)(2,1)} %cx_ref.1, bf16[48,256]{1,0:T(8,128)(2,1)} %cw_ref.1), custom_call_target="tpu_custom_call" | custom-call | tf_op jit(solution)/shard_map/pallas_call | solution.py:39
  2.1 7.2 %collective-permute-start.6 = (bf16[64,256]{1,0:T(8,128)(2,1)}, bf16[64,256]{1,0:T(8,128)(2,1)S(1)}, u32[]{:S(2)}, u32[]{:S(2)}) collective-permute-start(bf16[64,256]{1,0:T(8,128)(2,1)} %get-tuple-element.8), channel_id=1, source_target_pairs={{0,32},{16,48},{32,0},{48,16},{64,96},{80,112},{96,64},{112,80},{1... | collective-permute-start | bytes 98312 | tf_op jit(solution)/shard_map/ppermute | solution.py:118
  9.3 1.9 %collective-permute-start.2 = (bf16[64,256]{1,0:T(8,128)(2,1)}, bf16[64,256]{1,0:T(8,128)(2,1)S(1)}, u32[]{:S(2)}, u32[]{:S(2)}) collective-permute-start(bf16[64,256]{1,0:T(8,128)(2,1)} %get-tuple-element.7), channel_id=1, source_target_pairs={{0,3},{1,0},{2,1},{3,2},{4,7},{5,4},{6,5},{7,6},{8,11},{9,8},{10,9... | collective-permute-start | bytes 98312 | tf_op jit(solution)/shard_map/ppermute | solution.py:118
  11.2 0.6 collective-permute-start.1
  11.7 1.0 collective-permute-start
  12.8 0.8 pad_maximum_fusion.1.refs_4_
  14.1 2.6 %collective-permute-start.8 = (bf16[2,64,256]{2,1,0:T(8,128)(2,1)S(1)}, bf16[2,64,256]{2,1,0:T(8,128)(2,1)S(1)}, u32[]{:S(2)}, u32[]{:S(2)}) collective-permute-start(bf16[2,64,256]{2,1,0:T(8,128)(2,1)S(1)} %pad_maximum_fusion.1.refs_4_), channel_id=1, source_target_pairs={{0,128},{16,144},{32,160},{48,176},{64,192},{80,208},{96,224},{112... | collective-permute-start | bytes 196616 | tf_op jit(solution)/shard_map/ppermute | solution.py:118
  16.7 1.9 %collective-permute-start.7 = (bf16[2,64,256]{2,1,0:T(8,128)(2,1)S(1)}, bf16[2,64,256]{2,1,0:T(8,128)(2,1)S(1)}, u32[]{:S(2)}, u32[]{:S(2)}) collective-permute-start(bf16[2,64,256]{2,1,0:T(8,128)(2,1)S(1)} %pad_maximum_fusion.1.refs_4_), channel_id=1, source_target_pairs={{0,64},{16,80},{32,96},{48,112},{64,128},{80,144},{96,160},{112,17... | collective-permute-start | bytes 196616 | tf_op jit(solution)/shard_map/ppermute | solution.py:118
  18.6 2.8 %collective-permute-start.5 = (bf16[4,64,256]{2,1,0:T(8,128)(2,1)S(1)}, bf16[4,64,256]{2,1,0:T(8,128)(2,1)S(1)}, u32[]{:S(2)}, u32[]{:S(2)}) collective-permute-start(bf16[4,64,256]{2,1,0:T(8,128)(2,1)S(1)} %pad_maximum_fusion.refs_0_), channel_id=1, source_target_pairs={{0,12},{1,13},{2,14},{3,15},{4,0},{5,1},{6,2},{7,3},{8,4},{9,5},{1... | collective-permute-start | bytes 393224 | tf_op jit(solution)/shard_map/ppermute | solution.py:118
  21.4 0.9 collective-permute-start.4
  22.3 0.9 collective-permute-start.3
  23.7 0.7 collective-permute-done.12.refs_10_
  24.6 2.2 %collective-permute-done.5.refs_3_ = bf16[4,64,256]{2,1,0:T(8,128)(2,1)S(1)} collective-permute-done((bf16[4,64,256]{2,1,0:T(8,128)(2,1)S(1)}, bf16[4,64,256]{2,1,0:T(8,128)(2,1)S(1)}, u32[]{:S(2)}, u32[]{:S(2)}) %collective-permute-start.5) | collective-permute-done | bytes 131104 | tf_op jit(solution)/shard_map/ppermute | solution.py:118
  26.8 2.6 %collective-permute-done.4.refs_2_ = bf16[4,64,256]{2,1,0:T(8,128)(2,1)S(1)} collective-permute-done((bf16[4,64,256]{2,1,0:T(8,128)(2,1)S(1)}, bf16[4,64,256]{2,1,0:T(8,128)(2,1)S(1)}, u32[]{:S(2)}, u32[]{:S(2)}) %collective-permute-start.4) | collective-permute-done | bytes 131104 | tf_op jit(solution)/shard_map/ppermute | solution.py:118
  29.4 2.3 %collective-permute-done.3.refs_1_ = bf16[4,64,256]{2,1,0:T(8,128)(2,1)S(1)} collective-permute-done((bf16[4,64,256]{2,1,0:T(8,128)(2,1)S(1)}, bf16[4,64,256]{2,1,0:T(8,128)(2,1)S(1)}, u32[]{:S(2)}, u32[]{:S(2)}) %collective-permute-start.3) | collective-permute-done | bytes 131104 | tf_op jit(solution)/shard_map/ppermute | solution.py:118
  31.7 45.7 %shard_map.68 = (f32[16,56,256]{2,1,0:T(8,128)S(1)}, f32[16,8,256]{2,1,0:T(8,128)S(1)}) custom-call(bf16[4,64,256]{2,1,0:T(8,128)(2,1)S(1)} %pad_maximum_fusion.refs_0_, bf16[4,64,256]{2,1,0:T(8,128)(2,1)S(1)} %collective-permute-done.3.refs_1_, bf16[4,64,256]{2,1,0:T(8,128)(2,1)S(1)} %collective-permute-done.4.refs_2_, ...), custom_call_target="tpu_custom_call" | custom-call | flops 10000000000 | bytes 4000000 | tf_op jit(solution)/shard_map/pallas_call | solution.py:97
  77.8 0.7 collective-permute-start.19
  78.4 1.4 %collective-permute-start.21 = (f32[4,8,256]{2,1,0:T(8,128)S(1)}, f32[4,8,256]{2,1,0:T(8,128)S(1)}, u32[]{:S(2)}, u32[]{:S(2)}) collective-permute-start(f32[4,8,256]{2,1,0:T(8,128)S(1)} %get-tuple-element.15), channel_id=1, source_target_pairs={{0,4},{1,5},{2,6},{3,7},{4,8},{5,9},{6,10},{7,11},{8,12},{9,13},{1... | collective-permute-start | bytes 98312 | tf_op jit(solution)/shard_map/ppermute | solution.py:118
  79.9 0.9 collective-permute-start.20
  80.8 1.0 collective-permute-done.19
  81.7 1.8 %collective-permute-done.21 = f32[4,8,256]{2,1,0:T(8,128)S(1)} collective-permute-done((f32[4,8,256]{2,1,0:T(8,128)S(1)}, f32[4,8,256]{2,1,0:T(8,128)S(1)}, u32[]{:S(2)}, u32[]{:S(2)}) %collective-permute-start.21) | collective-permute-done | bytes 32800 | tf_op jit(solution)/shard_map/ppermute | solution.py:118
  83.6 1.7 %collective-permute-done.20 = f32[4,8,256]{2,1,0:T(8,128)S(1)} collective-permute-done((f32[4,8,256]{2,1,0:T(8,128)S(1)}, f32[4,8,256]{2,1,0:T(8,128)S(1)}, u32[]{:S(2)}, u32[]{:S(2)}) %collective-permute-start.20) | collective-permute-done | bytes 32800 | tf_op jit(solution)/shard_map/ppermute | solution.py:118
  85.7 1.8 %collective-permute-start.17 = (f32[2,56,256]{2,1,0:T(8,128)S(1)}, f32[2,56,256]{2,1,0:T(8,128)S(1)}, u32[]{:S(2)}, u32[]{:S(2)}) collective-permute-start(f32[2,56,256]{2,1,0:T(8,128)S(1)} %get-tuple-element.12), channel_id=1, source_target_pairs={{0,64},{16,80},{32,96},{48,112},{64,128},{80,144},{96,160},{112,17... | collective-permute-start | bytes 344072 | tf_op jit(solution)/shard_map/ppermute | solution.py:118
  87.5 2.9 %collective-permute-start.16 = (f32[2,56,256]{2,1,0:T(8,128)S(1)}, f32[2,56,256]{2,1,0:T(8,128)S(1)}, u32[]{:S(2)}, u32[]{:S(2)}) collective-permute-start(f32[2,56,256]{2,1,0:T(8,128)S(1)} %get-tuple-element.13), channel_id=1, source_target_pairs={{0,128},{16,144},{32,160},{48,176},{64,192},{80,208},{96,224},{112... | collective-permute-start | bytes 344072 | tf_op jit(solution)/shard_map/ppermute | solution.py:118
  90.4 1.8 %collective-permute-start.24 = (f32[8,256]{1,0:T(8,128)S(1)}, f32[8,256]{1,0:T(8,128)S(1)}, u32[]{:S(2)}, u32[]{:S(2)}) collective-permute-start(f32[8,256]{1,0:T(8,128)S(1)} %get-tuple-element.18), channel_id=1, source_target_pairs={{0,1},{1,2},{2,3},{3,0},{4,5},{5,6},{6,7},{7,4},{8,9},{9,10},{10,1... | collective-permute-start | bytes 24584 | tf_op jit(solution)/shard_map/ppermute | solution.py:118
  92.2 1.5 %collective-permute-start.23 = (f32[8,256]{1,0:T(8,128)S(1)}, f32[8,256]{1,0:T(8,128)S(1)}, u32[]{:S(2)}, u32[]{:S(2)}) collective-permute-start(f32[8,256]{1,0:T(8,128)S(1)} %get-tuple-element.19), channel_id=1, source_target_pairs={{0,2},{1,3},{2,0},{3,1},{4,6},{5,7},{6,4},{7,5},{8,10},{9,11},{10,... | collective-permute-start | bytes 24584 | tf_op jit(solution)/shard_map/ppermute | solution.py:118
  93.7 1.1 %collective-permute-start.22 = (f32[8,256]{1,0:T(8,128)S(1)}, f32[8,256]{1,0:T(8,128)S(1)}, u32[]{:S(2)}, u32[]{:S(2)}) collective-permute-start(f32[8,256]{1,0:T(8,128)S(1)} %get-tuple-element.20), channel_id=1, source_target_pairs={{0,3},{1,0},{2,1},{3,2},{4,7},{5,4},{6,5},{7,6},{8,11},{9,8},{10,9... | collective-permute-start | bytes 24584 | tf_op jit(solution)/shard_map/ppermute | solution.py:118
  94.8 4.9 %collective-permute-start.18 = (f32[56,256]{1,0:T(8,128)S(1)}, f32[56,256]{1,0:T(8,128)S(1)}, u32[]{:S(2)}, u32[]{:S(2)}) collective-permute-start(f32[56,256]{1,0:T(8,128)S(1)} %slice_bitcast_fusion), channel_id=1, source_target_pairs={{0,32},{16,48},{32,0},{48,16},{64,96},{80,112},{96,64},{112,80},{1... | collective-permute-start | bytes 172040 | tf_op jit(solution)/shard_map/ppermute | solution.py:118
  99.7 0.6 slice_add_fusion.2
  100.3 2.7 %collective-permute-done.18 = f32[56,256]{1,0:T(8,128)S(1)} collective-permute-done((f32[56,256]{1,0:T(8,128)S(1)}, f32[56,256]{1,0:T(8,128)S(1)}, u32[]{:S(2)}, u32[]{:S(2)}) %collective-permute-start.18) | collective-permute-done | bytes 57376 | tf_op jit(solution)/shard_map/ppermute | solution.py:118
  103.0 0.6 slice.91
  103.6 0.6 slice.82
  (36 shorter events, 2.1 us)
Async XLA Ops:
  2.1 10.7 %collective-permute-start.6 = (bf16[64,256]{1,0:T(8,128)(2,1)}, bf16[64,256]{1,0:T(8,128)(2,1)S(1)}, u32[]{:S(2)}, u32[]{:S(2)}) collective-permute-start(bf16[64,256]{1,0:T(8,128)(2,1)} %get-tuple-element.8), channel_id=1, source_target_pairs={{0,32},{16,48},{32,0},{48,16},{64,96},{80,112},{96,64},{112,80},{1... | collective-permute-start | bytes 98312 | tf_op jit(solution)/shard_map/ppermute | solution.py:118
  9.3 4.8 %collective-permute-start.2 = (bf16[64,256]{1,0:T(8,128)(2,1)}, bf16[64,256]{1,0:T(8,128)(2,1)S(1)}, u32[]{:S(2)}, u32[]{:S(2)}) collective-permute-start(bf16[64,256]{1,0:T(8,128)(2,1)} %get-tuple-element.7), channel_id=1, source_target_pairs={{0,3},{1,0},{2,1},{3,2},{4,7},{5,4},{6,5},{7,6},{8,11},{9,8},{10,9... | collective-permute-start | bytes 98312 | tf_op jit(solution)/shard_map/ppermute | solution.py:118
  11.2 5.5 %collective-permute-start.1 = (bf16[64,256]{1,0:T(8,128)(2,1)}, bf16[64,256]{1,0:T(8,128)(2,1)S(1)}, u32[]{:S(2)}, u32[]{:S(2)}) collective-permute-start(bf16[64,256]{1,0:T(8,128)(2,1)} %get-tuple-element.7), channel_id=1, source_target_pairs={{0,2},{1,3},{2,0},{3,1},{4,6},{5,7},{6,4},{7,5},{8,10},{9,11},{10,... | collective-permute-start | bytes 98312 | tf_op jit(solution)/shard_map/ppermute | solution.py:118
  11.7 6.8 %collective-permute-start = (bf16[64,256]{1,0:T(8,128)(2,1)}, bf16[64,256]{1,0:T(8,128)(2,1)S(1)}, u32[]{:S(2)}, u32[]{:S(2)}) collective-permute-start(bf16[64,256]{1,0:T(8,128)(2,1)} %get-tuple-element.7), channel_id=1, source_target_pairs={{0,1},{1,2},{2,3},{3,0},{4,5},{5,6},{6,7},{7,4},{8,9},{9,10},{10,1... | collective-permute-start | bytes 98312 | tf_op jit(solution)/shard_map/ppermute | solution.py:118
  12.8 5.8 %copy-start = (bf16[64,256]{1,0:T(8,128)(2,1)S(1)}, bf16[64,256]{1,0:T(8,128)(2,1)}, u32[]{:S(2)}) copy-start(bf16[64,256]{1,0:T(8,128)(2,1)} %get-tuple-element.7) | copy-start | bytes 98308
  13.5 7.9 %collective-permute-start.10 = (bf16[2,64,256]{2,1,0:T(8,128)(2,1)S(1)}, bf16[2,64,256]{2,1,0:T(8,128)(2,1)S(1)}, u32[]{:S(2)}, u32[]{:S(2)}) collective-permute-start(bf16[2,64,256]{2,1,0:T(8,128)(2,1)S(1)} %pad_maximum_fusion.1.refs_4_), channel_id=1, source_target_pairs={{0,16},{16,0},{32,48},{48,32},{64,80},{80,64},{96,112},{112,96},{1... | collective-permute-start | bytes 196616 | tf_op jit(solution)/shard_map/ppermute | solution.py:118
  13.6 7.9 %collective-permute-start.9 = (bf16[2,64,256]{2,1,0:T(8,128)(2,1)S(1)}, bf16[2,64,256]{2,1,0:T(8,128)(2,1)S(1)}, u32[]{:S(2)}, u32[]{:S(2)}) collective-permute-start(bf16[2,64,256]{2,1,0:T(8,128)(2,1)S(1)} %pad_maximum_fusion.1.refs_4_), channel_id=1, source_target_pairs={{0,192},{16,208},{32,224},{48,240},{64,0},{80,16},{96,32},{112,48}... | collective-permute-start | bytes 196616 | tf_op jit(solution)/shard_map/ppermute | solution.py:118
  14.1 8.2 %collective-permute-start.8 = (bf16[2,64,256]{2,1,0:T(8,128)(2,1)S(1)}, bf16[2,64,256]{2,1,0:T(8,128)(2,1)S(1)}, u32[]{:S(2)}, u32[]{:S(2)}) collective-permute-start(bf16[2,64,256]{2,1,0:T(8,128)(2,1)S(1)} %pad_maximum_fusion.1.refs_4_), channel_id=1, source_target_pairs={{0,128},{16,144},{32,160},{48,176},{64,192},{80,208},{96,224},{112... | collective-permute-start | bytes 196616 | tf_op jit(solution)/shard_map/ppermute | solution.py:118
  16.7 6.5 %collective-permute-start.7 = (bf16[2,64,256]{2,1,0:T(8,128)(2,1)S(1)}, bf16[2,64,256]{2,1,0:T(8,128)(2,1)S(1)}, u32[]{:S(2)}, u32[]{:S(2)}) collective-permute-start(bf16[2,64,256]{2,1,0:T(8,128)(2,1)S(1)} %pad_maximum_fusion.1.refs_4_), channel_id=1, source_target_pairs={{0,64},{16,80},{32,96},{48,112},{64,128},{80,144},{96,160},{112,17... | collective-permute-start | bytes 196616 | tf_op jit(solution)/shard_map/ppermute | solution.py:118
  18.6 8.2 %collective-permute-start.5 = (bf16[4,64,256]{2,1,0:T(8,128)(2,1)S(1)}, bf16[4,64,256]{2,1,0:T(8,128)(2,1)S(1)}, u32[]{:S(2)}, u32[]{:S(2)}) collective-permute-start(bf16[4,64,256]{2,1,0:T(8,128)(2,1)S(1)} %pad_maximum_fusion.refs_0_), channel_id=1, source_target_pairs={{0,12},{1,13},{2,14},{3,15},{4,0},{5,1},{6,2},{7,3},{8,4},{9,5},{1... | collective-permute-start | bytes 393224 | tf_op jit(solution)/shard_map/ppermute | solution.py:118
  21.4 1.8 %collective-permute-start.13 = (bf16[2,64,256]{2,1,0:T(8,128)(2,1)S(1)}, bf16[2,64,256]{2,1,0:T(8,128)(2,1)S(1)}, u32[]{:S(2)}, u32[]{:S(2)}) collective-permute-start(bf16[2,64,256]{2,1,0:T(8,128)(2,1)S(1)} %collective-permute-done.9.refs_7_), channel_id=1, source_target_pairs={{0,16},{16,0},{32,48},{48,32},{64,80},{80,64},{96,112},{112,96},{1... | collective-permute-start | bytes 196616 | tf_op jit(solution)/shard_map/ppermute | solution.py:118
  21.4 7.9 %collective-permute-start.4 = (bf16[4,64,256]{2,1,0:T(8,128)(2,1)S(1)}, bf16[4,64,256]{2,1,0:T(8,128)(2,1)S(1)}, u32[]{:S(2)}, u32[]{:S(2)}) collective-permute-start(bf16[4,64,256]{2,1,0:T(8,128)(2,1)S(1)} %pad_maximum_fusion.refs_0_), channel_id=1, source_target_pairs={{0,8},{1,9},{2,10},{3,11},{4,12},{5,13},{6,14},{7,15},{8,0},{9,1},... | collective-permute-start | bytes 393224 | tf_op jit(solution)/shard_map/ppermute | solution.py:118
  22.3 9.3 %collective-permute-start.3 = (bf16[4,64,256]{2,1,0:T(8,128)(2,1)S(1)}, bf16[4,64,256]{2,1,0:T(8,128)(2,1)S(1)}, u32[]{:S(2)}, u32[]{:S(2)}) collective-permute-start(bf16[4,64,256]{2,1,0:T(8,128)(2,1)S(1)} %pad_maximum_fusion.refs_0_), channel_id=1, source_target_pairs={{0,4},{1,5},{2,6},{3,7},{4,8},{5,9},{6,10},{7,11},{8,12},{9,13},{1... | collective-permute-start | bytes 393224 | tf_op jit(solution)/shard_map/ppermute | solution.py:118
  23.2 1.3 %collective-permute-start.12 = (bf16[2,64,256]{2,1,0:T(8,128)(2,1)S(1)}, bf16[2,64,256]{2,1,0:T(8,128)(2,1)S(1)}, u32[]{:S(2)}, u32[]{:S(2)}) collective-permute-start(bf16[2,64,256]{2,1,0:T(8,128)(2,1)S(1)} %collective-permute-done.8.refs_6_), channel_id=1, source_target_pairs={{0,16},{16,0},{32,48},{48,32},{64,80},{80,64},{96,112},{112,96},{1... | collective-permute-start | bytes 196616 | tf_op jit(solution)/shard_map/ppermute | solution.py:118
  23.2 1.4 %collective-permute-start.11 = (bf16[2,64,256]{2,1,0:T(8,128)(2,1)S(1)}, bf16[2,64,256]{2,1,0:T(8,128)(2,1)S(1)}, u32[]{:S(2)}, u32[]{:S(2)}) collective-permute-start(bf16[2,64,256]{2,1,0:T(8,128)(2,1)S(1)} %collective-permute-done.7.refs_5_), channel_id=1, source_target_pairs={{0,16},{16,0},{32,48},{48,32},{64,80},{80,64},{96,112},{112,96},{1... | collective-permute-start | bytes 196616 | tf_op jit(solution)/shard_map/ppermute | solution.py:118
  77.4 7.8 %collective-permute-start.14 = (f32[8,56,256]{2,1,0:T(8,128)S(1)}, f32[8,56,256]{2,1,0:T(8,128)S(1)}, u32[]{:S(2)}, u32[]{:S(2)}) collective-permute-start(f32[8,56,256]{2,1,0:T(8,128)S(1)} %slice.58), channel_id=1, source_target_pairs={{0,16},{16,0},{32,48},{48,32},{64,80},{80,64},{96,112},{112,96},{1... | collective-permute-start | bytes 1376264 | tf_op jit(solution)/shard_map/ppermute | solution.py:118
  77.8 4.0 %collective-permute-start.19 = (f32[4,8,256]{2,1,0:T(8,128)S(1)}, f32[4,8,256]{2,1,0:T(8,128)S(1)}, u32[]{:S(2)}, u32[]{:S(2)}) collective-permute-start(f32[4,8,256]{2,1,0:T(8,128)S(1)} %get-tuple-element.14), channel_id=1, source_target_pairs={{0,12},{1,13},{2,14},{3,15},{4,0},{5,1},{6,2},{7,3},{8,4},{9,5},{1... | collective-permute-start | bytes 98312 | tf_op jit(solution)/shard_map/ppermute | solution.py:118
  78.4 5.1 %collective-permute-start.21 = (f32[4,8,256]{2,1,0:T(8,128)S(1)}, f32[4,8,256]{2,1,0:T(8,128)S(1)}, u32[]{:S(2)}, u32[]{:S(2)}) collective-permute-start(f32[4,8,256]{2,1,0:T(8,128)S(1)} %get-tuple-element.15), channel_id=1, source_target_pairs={{0,4},{1,5},{2,6},{3,7},{4,8},{5,9},{6,10},{7,11},{8,12},{9,13},{1... | collective-permute-start | bytes 98312 | tf_op jit(solution)/shard_map/ppermute | solution.py:118
  79.9 5.4 %collective-permute-start.20 = (f32[4,8,256]{2,1,0:T(8,128)S(1)}, f32[4,8,256]{2,1,0:T(8,128)S(1)}, u32[]{:S(2)}, u32[]{:S(2)}) collective-permute-start(f32[4,8,256]{2,1,0:T(8,128)S(1)} %get-tuple-element.16), channel_id=1, source_target_pairs={{0,8},{1,9},{2,10},{3,11},{4,12},{5,13},{6,14},{7,15},{8,0},{9,1},... | collective-permute-start | bytes 98312 | tf_op jit(solution)/shard_map/ppermute | solution.py:118
  85.4 8.3 %collective-permute-start.15 = (f32[2,56,256]{2,1,0:T(8,128)S(1)}, f32[2,56,256]{2,1,0:T(8,128)S(1)}, u32[]{:S(2)}, u32[]{:S(2)}) collective-permute-start(f32[2,56,256]{2,1,0:T(8,128)S(1)} %get-tuple-element.11), channel_id=1, source_target_pairs={{0,192},{16,208},{32,224},{48,240},{64,0},{80,16},{96,32},{112,48}... | collective-permute-start | bytes 344072 | tf_op jit(solution)/shard_map/ppermute | solution.py:118
  85.7 9.0 %collective-permute-start.17 = (f32[2,56,256]{2,1,0:T(8,128)S(1)}, f32[2,56,256]{2,1,0:T(8,128)S(1)}, u32[]{:S(2)}, u32[]{:S(2)}) collective-permute-start(f32[2,56,256]{2,1,0:T(8,128)S(1)} %get-tuple-element.12), channel_id=1, source_target_pairs={{0,64},{16,80},{32,96},{48,112},{64,128},{80,144},{96,160},{112,17... | collective-permute-start | bytes 344072 | tf_op jit(solution)/shard_map/ppermute | solution.py:118
  87.5 7.3 %collective-permute-start.16 = (f32[2,56,256]{2,1,0:T(8,128)S(1)}, f32[2,56,256]{2,1,0:T(8,128)S(1)}, u32[]{:S(2)}, u32[]{:S(2)}) collective-permute-start(f32[2,56,256]{2,1,0:T(8,128)S(1)} %get-tuple-element.13), channel_id=1, source_target_pairs={{0,128},{16,144},{32,160},{48,176},{64,192},{80,208},{96,224},{112... | collective-permute-start | bytes 344072 | tf_op jit(solution)/shard_map/ppermute | solution.py:118
  90.4 9.3 %collective-permute-start.24 = (f32[8,256]{1,0:T(8,128)S(1)}, f32[8,256]{1,0:T(8,128)S(1)}, u32[]{:S(2)}, u32[]{:S(2)}) collective-permute-start(f32[8,256]{1,0:T(8,128)S(1)} %get-tuple-element.18), channel_id=1, source_target_pairs={{0,1},{1,2},{2,3},{3,0},{4,5},{5,6},{6,7},{7,4},{8,9},{9,10},{10,1... | collective-permute-start | bytes 24584 | tf_op jit(solution)/shard_map/ppermute | solution.py:118
  92.2 7.5 %collective-permute-start.23 = (f32[8,256]{1,0:T(8,128)S(1)}, f32[8,256]{1,0:T(8,128)S(1)}, u32[]{:S(2)}, u32[]{:S(2)}) collective-permute-start(f32[8,256]{1,0:T(8,128)S(1)} %get-tuple-element.19), channel_id=1, source_target_pairs={{0,2},{1,3},{2,0},{3,1},{4,6},{5,7},{6,4},{7,5},{8,10},{9,11},{10,... | collective-permute-start | bytes 24584 | tf_op jit(solution)/shard_map/ppermute | solution.py:118
  93.7 6.0 %collective-permute-start.22 = (f32[8,256]{1,0:T(8,128)S(1)}, f32[8,256]{1,0:T(8,128)S(1)}, u32[]{:S(2)}, u32[]{:S(2)}) collective-permute-start(f32[8,256]{1,0:T(8,128)S(1)} %get-tuple-element.20), channel_id=1, source_target_pairs={{0,3},{1,0},{2,1},{3,2},{4,7},{5,4},{6,5},{7,6},{8,11},{9,8},{10,9... | collective-permute-start | bytes 24584 | tf_op jit(solution)/shard_map/ppermute | solution.py:118
  94.8 8.2 %collective-permute-start.18 = (f32[56,256]{1,0:T(8,128)S(1)}, f32[56,256]{1,0:T(8,128)S(1)}, u32[]{:S(2)}, u32[]{:S(2)}) collective-permute-start(f32[56,256]{1,0:T(8,128)S(1)} %slice_bitcast_fusion), channel_id=1, source_target_pairs={{0,32},{16,48},{32,0},{48,16},{64,96},{80,112},{96,64},{112,80},{1... | collective-permute-start | bytes 172040 | tf_op jit(solution)/shard_map/ppermute | solution.py:118
